TPU v7x, 512 devices: a whole 4x8x8 slice. The times are simulated.
512 devices in a mesh: row: 32 (over y, x), col: 16 (over z, core).
Axes of the slice: x: 4, y: 8, z: 8, core: 2. Of those that a mesh axis runs over, the one named last changes fastest.
Arguments:
- resident_inverse: bfloat16 [24576, 24576], P('row', 'col')
- factor: bfloat16 [3, 24576, 512], P(None, 'row', 'col'), may hold values from -0.4375 to 0.4375
- diag_inverse: float32 [3, 512, 512], P(None, None, 'col'), may hold values from -4 to 4
- anc_tiles: int32 [3, 64], replicated, may hold values from -1 to 95, as said below
- slot_tile: int32 [96], replicated, may hold values from 0 to 95, as said below
Outputs:
- new_cols: bfloat16 [3, 24576, 512], P(None, 'row', 'col')
- diag_blocks: float32 [3, 512, 512], P(None, None, 'col')
Inputs may be any that keep to these rules, and one draw needn't show every extreme that they name: `anc_tiles`: row j lists the ancestor tiles of supernode j in ascending order, each at most once, followed by -1 in unused entries; every list holds tile 96 - 1; list 0 is full and list 2 has fewer than 32 tiles. A permutation of the tiles; slot s holds tile slot_tile[s], and each tile is stored within the same block of 6 consecutive slots as its own index. `resident_inverse` is symmetric.
All inputs are finite; a program needn't handle non-finite values.
Results may differ from a plain program's by a relative error of at most 0.017.
Values may be sent and summed in bfloat16 or wider, within the bound.
No kernel may reach another device: no remote copies, remote signals or barrier semaphores. Data moves between devices by JAX's collectives and lax.ppermute only.
A program may use at most 64 MiB of HBM per device.

v0:
```python
import jax
import jax.numpy as jnp
from jax import lax
from jax.sharding import PartitionSpec as P


def broadcast(array, axis, root):
    mine = lax.axis_index(axis) == root
    return lax.psum(jnp.where(mine, array, jnp.zeros_like(array)), axis)


def slot_rows(anc_tiles, slot_tile, tile_rows):
    tile_count = slot_tile.shape[0]
    tile_ids = jnp.arange(tile_count, dtype=jnp.int32)
    listed = jnp.sum((anc_tiles[:, :, None] == tile_ids[None, None, :]).astype(jnp.float32), axis=1)
    onehot = (slot_tile[:, None] == tile_ids[None, :]).astype(jnp.float32)
    slot_mask = jnp.dot(listed, onehot.T, precision=lax.Precision.HIGHEST)
    return jnp.repeat(slot_mask, tile_rows, axis=1)


def on_device(resident_inverse, factor, diag_inverse, anc_tiles, slot_tile):
    own_rows = resident_inverse.shape[0]
    row_index = lax.axis_index("row")
    col_index = lax.axis_index("col")
    col_count = lax.axis_size("col")
    row_count = lax.axis_size("row")
    total_rows = own_rows * row_count
    row_mask = slot_rows(anc_tiles, slot_tile, total_rows // slot_tile.shape[0])
    own_mask = lax.dynamic_slice_in_dim(row_mask, row_index * own_rows, own_rows, 1)
    full_width = lax.all_gather(factor, "col", axis=2, tiled=True)
    masked_rows = full_width * own_mask.astype(jnp.bfloat16)[:, :, None]
    ratio = row_count // col_count
    pieces = []
    for within in range(ratio):
        pieces.append(broadcast(masked_rows, "row", col_index * ratio + within))
    masked_cols = jnp.concatenate(pieces, axis=1)
    partial_value = jnp.einsum(
        "rk,skw->srw", resident_inverse, masked_cols, preferred_element_type=jnp.float32
    )
    summed = lax.psum_scatter(
        partial_value.astype(jnp.bfloat16), "col", scatter_dimension=2, tiled=True
    ).astype(jnp.float32)
    new_cols = (-(summed * own_mask[:, :, None])).astype(jnp.bfloat16)
    contrib = jnp.einsum(
        "srw,srv->swv", masked_rows.astype(jnp.float32), summed, precision=lax.Precision.HIGHEST
    )
    totals = lax.psum(contrib.astype(jnp.bfloat16), "row").astype(jnp.float32)
    diag_blocks = diag_inverse + totals
    return (new_cols, diag_blocks)


def solution(mesh):
    placed = (P("row", "col"), P(None, "row", "col"), P(None, None, "col"), P(), P())
    return jax.shard_map(
        on_device,
        mesh=mesh,
        in_specs=placed,
        out_specs=(P(None, "row", "col"), P(None, None, "col")),
        check_vma=False,
    )
```

profile of v0, /device:TPU:64, one launch (start us, length us, event | category | flops | bytes accessed | tf_op | source)
XLA Modules:
  0.0 469.3 jit_solution(12427480146981224497)
XLA Ops:
  7.2 0.0 copy-start
  7.2 0.0 all-gather.2.cloned.1.call-start
  7.2 0.7 all-gather.2.cloned.1.call-update
  7.9 0.0 all-reduce.6.cloned.1.call-start
  8.0 0.8 convert_reduce_fusion
  8.8 0.8 fusion.15
  9.6 0.2 broadcast_bitcast_fusion
  9.8 0.2 copy.10
  10.0 46.5 %all-gather.2.cloned.1.call-done = bf16[3,768,512]{1,2,0:T(8,128)(2,1)} async-done(((bf16[3,768,32]{1,2,0:T(8,128)(2,1)}), bf16[3,768,512]{1,2,0:T(8,128)(2,1)}) %all-gather.2.cloned.1.call-update) | async-done | bytes 2359312 | tf_op jit(solution)/shard_map/all_gather | solution.py:30
  56.5 4.2 broadcast_select_fusion.1
  60.7 0.0 all-reduce.6.cloned.1.call-update
  60.7 0.0 reduce-scatter.2.cloned.1.call-start
  60.7 177.5 %all-reduce.6.cloned.1.call-done = (bf16[3,768,512]{1,2,0:T(8,128)(2,1)}, bf16[3,768,512]{1,2,0:T(8,128)(2,1)}) async-done(((bf16[3,768,512]{1,2,0:T(8,128)(2,1)}, bf16[3,768,512]{1,2,0:T(8,128)(2,1)}), (bf16[3,768,512]{1,2,0:T(8,128)(2,1)}, bf16[3,768,512]{1,2,0:T(8,128)(2,1)})) %all-reduce.6.cloned.1.call-update) | async-done | bytes 4718608 | tf_op jit(solution)/shard_map/psum | solution.py:9
  238.2 0.0 copy-done
  238.2 7.7 %convert_bitcast_fusion = bf16[3,768,512]{1,2,0:T(8,128)(2,1)} fusion(bf16[768,1536]{1,0:T(8,128)(2,1)S(1)} %copy-done, bf16[3,768,512]{1,2,0:T(8,128)(2,1)} %get-tuple-element.2, bf16[3,768,512]{1,2,0:T(8,128)(2,1)} %get-tuple-element.3), kind=kOutput, calls=%fused_computation.5 | convolution fusion | flops 3634495488 | bytes 9437184 | tf_op jit(solution)/shard_map/rk,skw->srw/dot_general | solution.py:37
  245.9 0.0 reduce-scatter.2.cloned.1.call-update
  246.0 0.0 copy-start.1
  246.0 0.0 all-reduce.4.cloned.1.call-start
  246.0 57.8 %reduce-scatter.2.cloned.1.call-done = bf16[3,768,32]{1,2,0:T(8,128)(2,1)} async-done(((bf16[3,768,512]{1,2,0:T(8,128)(2,1)}), bf16[3,768,32]{1,2,0:T(8,128)(2,1)}) %reduce-scatter.2.cloned.1.call-update) | async-done | bytes 147472 | tf_op jit(solution)/shard_map/reduce_scatter | solution.py:40
  303.8 0.0 copy-start.2
  303.8 3.1 fusion.12
  307.0 0.0 all-reduce.4.cloned.1.call-update
  307.0 0.0 copy-done.2
  307.0 0.7 negate_convert_fusion
  307.7 153.5 %all-reduce.4.cloned.1.call-done = bf16[3,512,32]{1,2,0:T(8,128)(2,1)} async-done(((bf16[3,512,32]{1,2,0:T(8,128)(2,1)}), bf16[3,512,32]{1,2,0:T(8,128)(2,1)}) %all-reduce.4.cloned.1.call-update) | async-done | bytes 98320 | tf_op jit(solution)/shard_map/psum | solution.py:47
  461.2 0.0 copy-done.1
  461.2 1.6 convert_add_fusion
  (1 shorter events, 0.0 us)
Async XLA Ops:
  7.2 231.1 %copy-start = (bf16[768,1536]{1,0:T(8,128)(2,1)S(1)}, bf16[768,1536]{1,0:T(8,128)(2,1)}, u32[]{:S(2)}) copy-start(bf16[768,1536]{1,0:T(8,128)(2,1)} %param.5) | copy-start | bytes 7077892
  7.2 49.3 %all-gather.2.cloned.1.call-start = ((), (), s32[]{:S(2)}) async-start(), calls=%async_computation.1 | async-start | bytes 2506752 | tf_op jit(solution)/shard_map/all_gather | solution.py:30
  7.9 230.3 %all-reduce.6.cloned.1.call-start = ((), (), s32[]{:S(2)}) async-start(), calls=%async_computation.4 | async-start | bytes 9437184 | tf_op jit(solution)/shard_map/psum | solution.py:9
  60.7 243.1 %reduce-scatter.2.cloned.1.call-start = ((), (), s32[]{:S(2)}) async-start(), calls=%async_computation.2 | async-start | bytes 2506752 | tf_op jit(solution)/shard_map/reduce_scatter | solution.py:40
  246.0 215.2 %copy-start.1 = (f32[3,512,32]{1,2,0:T(8,128)S(1)}, f32[3,512,32]{1,2,0:T(8,128)}, u32[]{:S(2)}) copy-start(f32[3,512,32]{1,2,0:T(8,128)} %param.7) | copy-start | bytes 589828
  246.0 215.2 %all-reduce.4.cloned.1.call-start = ((), (), s32[]{:S(2)}) async-start(), calls=%async_computation.3 | async-start | bytes 196608 | tf_op jit(solution)/shard_map/psum | solution.py:47
  303.8 3.2 copy-start.2
Sparse Core Ops, SparseCore 0:
  10.2 46.2 all-gather.1
  60.8 177.3 all-reduce.5
  246.1 57.7 reduce-scatter.1
  308.0 153.1 all-reduce.3
where the time goes:
time: 470 us; the launch traced here: 469 us
  waiting for transfers between devices  436 us (93%)
  between operations  13.8 us (3%)
  matrix products  11.7 us (2%)
  other arithmetic  7.28 us (2%)
    psum x1, waiting for transfers between devices, broadcast(): return lax.psum(jnp.where(mine, array, jnp.zeros_like(array)), axis)  177 us
    psum x1, waiting for transfers between devices, on_device(): totals = lax.psum(contrib.astype(jnp.bfloat16), 'row').astype(jnp.float32)  153 us
    reduce_scatter x1, waiting for transfers between devices, on_device(): lax.psum_scatter(partial_value.astype(jnp.bfloat16), 'col', scatter_dimen...  57.8 us
    all_gather x1, waiting for transfers between devices, on_device(): full_width = lax.all_gather(factor, 'col', axis=2, tiled=True)  46.5 us
  transfers between devices with their start and end apart: 4, of which 4 were waited for; matrix products, arithmetic and copies ran while one was open for 1% of the time, Pallas kernels for 0%

commit v1 on v0

v1 whole, which is shorter than its diff:
```python
import jax
import jax.numpy as jnp
from jax import lax
from jax.experimental import pallas as pl
from jax.experimental.pallas import tpu as pltpu
from jax.sharding import Mesh, PartitionSpec as P

AXES = ("y", "x", "z", "k")
NY, NX, NZ, NK = 8, 4, 8, 2
SUPERS = 3
W = 512
WL = 32
ROWS = 768
SLOTS = 3
TB = 256


def linear(y, x, z, k):
    return ((y * NX + x) * NZ + z) * NK + k


def permutation(f):
    pairs = []
    for y in range(NY):
        for x in range(NX):
            for z in range(NZ):
                for k in range(NK):
                    pairs.append((linear(y, x, z, k), linear(*f(y, x, z, k))))
    return pairs


NT_DIMS = (((1,), (1,)), ((), ()))


def product_kernel(k_ref, g_ref, own_ref, sib_ref, m0_ref, m1_ref, m2_ref, part_ref, diag_ref, acc):
    step = pl.program_id(0)
    lhs = g_ref[...].reshape(NZ * SUPERS * WL, ROWS)

    @pl.when(step == 0)
    def _():
        acc[...] = lax.dot_general(lhs, own_ref[...], NT_DIMS, preferred_element_type=jnp.float32)

    @pl.when(step == 1)
    def _():
        acc[...] += lax.dot_general(lhs, own_ref[...], NT_DIMS, preferred_element_type=jnp.float32)

    @pl.when(step >= 2)
    def _():
        acc[...] += lax.dot_general(lhs, sib_ref[...], NT_DIMS, preferred_element_type=jnp.float32)

    @pl.when(step == 3)
    def _():
        part = acc[...].astype(jnp.bfloat16)
        part_ref[...] = part
        split = part.reshape(NZ, SUPERS, WL, ROWS)
        for j, m_ref in enumerate((m0_ref, m1_ref, m2_ref)):
            mine = split[:, j].reshape(NZ * WL, ROWS)
            diag = lax.dot_general(m_ref[...], mine, NT_DIMS, preferred_element_type=jnp.float32)
            diag_ref[:, j * NZ * WL:(j + 1) * NZ * WL] = diag.astype(jnp.bfloat16)


def products(core, gathered, own, sib, rows):
    n = NZ * SUPERS * WL

    def block_of(step, k_ref):
        side = jnp.where(step < 2, k_ref[0], 1 - k_ref[0])
        return 2 * side + step % 2

    whole = pl.BlockSpec((W, ROWS), lambda s, k: (0, 0))
    return pl.pallas_call(
        product_kernel,
        grid_spec=pltpu.PrefetchScalarGridSpec(
            num_scalar_prefetch=1,
            grid=(4,),
            in_specs=[
                pl.BlockSpec((NZ, 1, SUPERS * WL, ROWS), lambda s, k: (0, block_of(s, k), 0, 0)),
                pl.BlockSpec((ROWS, ROWS), lambda s, k: (0, jnp.minimum(s, 1))),
                pl.BlockSpec((ROWS, ROWS), lambda s, k: (0, jnp.maximum(s, 2) - 2)),
                whole, whole, whole,
            ],
            out_specs=[
                pl.BlockSpec((n, ROWS), lambda s, k: (0, 0)),
                pl.BlockSpec((W, n), lambda s, k: (0, 0)),
            ],
            scratch_shapes=[pltpu.VMEM((n, ROWS), jnp.float32)],
        ),
        out_shape=[
            jax.ShapeDtypeStruct((n, ROWS), jnp.bfloat16),
            jax.ShapeDtypeStruct((W, n), jnp.bfloat16),
        ],
        compiler_params=pltpu.CompilerParams(vmem_limit_bytes=44 * 1024 * 1024),
        cost_estimate=pl.CostEstimate(flops=4_900_000_000, bytes_accessed=14_000_000, transcendentals=0),
    )(core, gathered, own, sib, *rows)


def on_device(resident, factor, diag_inverse, anc_tiles, slot_tile):
    core = lax.axis_index("k")
    row = lax.axis_index("y") * NX + lax.axis_index("x")
    sib = lax.ppermute(resident, AXES, permutation(lambda y, x, z, k: (y, x, z, 1 - k)))

    slots = lax.dynamic_slice(slot_tile, (row * SLOTS,), (SLOTS,))
    listed = jnp.any(anc_tiles[:, None, :] == slots[None, :, None], axis=2)
    mask = jnp.repeat(listed, TB, axis=1)
    masked = jnp.where(mask[:, None, :], factor.transpose(0, 2, 1), jnp.bfloat16(0))
    flat = masked.reshape(SUPERS * WL, ROWS)

    moved = lax.ppermute(flat, AXES, permutation(lambda y, x, z, k: (z, x, y, k)))
    gathered = lax.all_gather(moved, ("y", "x"), axis=0, tiled=False)
    gathered = gathered.reshape(NZ, NX, SUPERS * WL, ROWS)
    rows = [lax.all_gather(masked[j], ("z", "k"), axis=0, tiled=True) for j in range(SUPERS)]

    part, diag = products(core.reshape(1), gathered, resident, sib, rows)

    summed = lax.psum_scatter(part, "z", scatter_dimension=0, tiled=True)
    summed = summed.reshape(SUPERS, WL, ROWS).astype(jnp.float32)
    new_cols = jnp.where(mask[:, None, :], -summed, 0.0).astype(jnp.bfloat16).transpose(0, 2, 1)

    spread = lax.all_to_all(diag.reshape(NY * NX, W // (NY * NX), SUPERS * NZ * WL), ("y", "x"), 0, 0, tiled=True)
    slab = jnp.sum(spread.astype(jnp.float32), axis=0).reshape(W // (NY * NX), SUPERS, NZ, WL)
    slab = slab.transpose(2, 0, 1, 3).reshape(NZ, W // (NY * NX), SUPERS * WL)
    slab = jnp.sum(lax.all_to_all(slab, "z", 0, 0, tiled=True), axis=0).astype(jnp.bfloat16)
    copies = jnp.broadcast_to(slab[None], (NY * NX,) + slab.shape)
    total = lax.all_to_all(copies, ("y", "x"), 0, 0, tiled=True)
    total = total.reshape(W, SUPERS, WL).transpose(1, 0, 2).astype(jnp.float32)
    return new_cols, diag_inverse + total


def solution(mesh):
    fine = Mesh(mesh.devices.reshape(NY, NX, NZ, NK), AXES)
    row, col = ("y", "x"), ("z", "k")
    return jax.shard_map(
        on_device,
        mesh=fine,
        in_specs=(P(row, col), P(None, row, col), P(None, None, col), P(), P()),
        out_specs=(P(None, row, col), P(None, None, col)),
        check_vma=False,
    )
```

time: 470 us -> 201 us (0.43)
  the two profiles are of different devices: /device:TPU:64 before, /device:TPU:8 now
where the time goes in v1:
time: 201 us; the launch traced here: 200 us
  blocking collectives  106 us (53%)
  waiting for transfers between devices  48.3 us (24%)
  between operations  14.2 us (7%)
  starting transfers between devices  12.2 us (6%)
  Pallas kernels  8.85 us (4%)
  local copies, waits for them, and re-layouts  5.89 us (3%)
  other arithmetic  4.79 us (2%)
    all_gather x3, blocking collectives, on_device(): lax.all_gather(masked[j], ('z', 'k'), axis=0, tiled=True)  65.3 us
    all_gather x1, waiting for transfers between devices, on_device(): gathered = lax.all_gather(moved, ('y', 'x'), axis=0, tiled=False)  29.7 us
    all_to_all x1, blocking collectives, on_device(): lax.all_to_all(diag.reshape(NY * NX, W // (NY * NX), SUPERS * NZ * WL), (...  25.2 us
    all_to_all x1, blocking collectives, on_device(): lax.all_to_all(slab, 'z', 0, 0, tiled=True)  15.8 us
    ppermute x1, waiting for transfers between devices, on_device(): lax.ppermute(flat, AXES, permutation(lambda y, x, z, k: (z, x, y, k)))  9.44 us
    all_to_all x1, waiting for transfers between devices, on_device(): total = lax.all_to_all(copies, ('y', 'x'), 0, 0, tiled=True)  9.15 us
    pallas_call x1, Pallas kernels, products(): pl.pallas_call(product_kernel, grid_spec=pltpu.PrefetchScalarGridSpec(num...  8.85 us
    all_to_all x1, starting transfers between devices, on_device(): total = lax.all_to_all(copies, ('y', 'x'), 0, 0, tiled=True)  5.99 us
  transfers between devices with their start and end apart: 5, of which 3 were waited for; matrix products, arithmetic and copies ran while one was open for 2% of the time, Pallas kernels for 0%

profile of v1, /device:TPU:8, one launch (start us, length us, event | category | flops | bytes accessed | tf_op | source)
XLA Modules:
  0.0 200.4 jit_solution(1800463783586215818)
XLA Ops:
  7.2 0.0 all-gather.6.cloned.1.call-start
  7.2 0.7 dynamic_slice.3
  7.9 0.9 compare_reduce_fusion
  8.8 0.1 broadcast_bitcast_fusion
  8.9 0.9 broadcast_select_fusion
  9.9 4.2 %collective-permute-start = (bf16[96,768]{1,0:T(8,128)(2,1)S(1)}, bf16[96,768]{1,0:T(8,128)(2,1)S(1)}, u32[]{:S(2)}, u32[]{:S(2)}) collective-permute-start(bf16[96,768]{1,0:T(8,128)(2,1)S(1)} %bitcast.25), channel_id=1, source_target_pairs={{0,0},{1,1},{2,64},{3,65},{4,128},{5,129},{6,192},{7,193},{8,256},... | collective-permute-start | bytes 442376 | tf_op jit(solution)/shard_map/ppermute | solution.py:107
  14.0 9.4 %collective-permute-done = bf16[96,768]{1,0:T(8,128)(2,1)S(1)} collective-permute-done((bf16[96,768]{1,0:T(8,128)(2,1)S(1)}, bf16[96,768]{1,0:T(8,128)(2,1)S(1)}, u32[]{:S(2)}, u32[]{:S(2)}) %collective-permute-start) | collective-permute-done | bytes 147488 | tf_op jit(solution)/shard_map/ppermute | solution.py:107
  23.5 0.0 copy-start.2
  23.5 0.7 copy-done.2
  24.1 0.0 all-gather.6.cloned.1.call-update
  24.2 0.0 reduce-scatter.2.cloned.1.call-start
  24.2 1.9 collective-permute-start.1
  26.1 0.9 fusion.2
  27.1 30.8 %all-gather.1 = bf16[1,512,768]{2,1,0:T(8,128)(2,1)S(1)} all-gather(bf16[1,32,768]{2,1,0:T(8,128)(2,1)S(1)} %get-tuple-element.14), channel_id=3, replica_groups=mesh['y'=8,'x'=4,'z'=8,'k'=2] {'z','k'}, dimensions={1}, use_global_device_ids=true | all-gather | bytes 835584 | tf_op jit(solution)/shard_map/all_gather | solution.py:110
  57.9 16.6 %all-gather.2 = bf16[1,512,768]{2,1,0:T(8,128)(2,1)S(1)} all-gather(bf16[1,32,768]{2,1,0:T(8,128)(2,1)S(1)} %get-tuple-element.13), channel_id=4, replica_groups=mesh['y'=8,'x'=4,'z'=8,'k'=2] {'z','k'}, dimensions={1}, use_global_device_ids=true | all-gather | bytes 835584 | tf_op jit(solution)/shard_map/all_gather | solution.py:110
  74.5 17.9 %all-gather.3 = bf16[1,512,768]{2,1,0:T(8,128)(2,1)S(1)} all-gather(bf16[1,32,768]{2,1,0:T(8,128)(2,1)S(1)} %get-tuple-element.12), channel_id=5, replica_groups=mesh['y'=8,'x'=4,'z'=8,'k'=2] {'z','k'}, dimensions={1}, use_global_device_ids=true | all-gather | bytes 835584 | tf_op jit(solution)/shard_map/all_gather | solution.py:110
  92.4 0.0 collective-permute-done.1.sib_ref
  92.4 29.7 %all-gather.6.cloned.1.call-done = bf16[3072,768]{1,0:T(8,128)(2,1)} async-done(((bf16[96,768]{1,0:T(8,128)(2,1)}), bf16[3072,768]{1,0:T(8,128)(2,1)}) %all-gather.6.cloned.1.call-update) | async-done | bytes 4718608 | tf_op jit(solution)/shard_map/all_gather | solution.py:108
  122.1 0.0 copy-start
  122.1 1.7 copy-done
  123.8 8.9 %shard_map.68 = (bf16[768,768]{1,0:T(8,128)(2,1)}, bf16[512,768]{1,0:T(8,128)(2,1)S(1)}) custom-call(s32[1]{0:T(128)} %bitcast.k_ref, bf16[8,4,96,768]{3,2,1,0:T(8,128)(2,1)} %bitcast.29, bf16[768,1536]{1,0:T(8,128)(2,1)S(1)} %copy-done, bf16[768,1536]{1,0:T(8,128)(2,1)} %collective-permute-done.1.sib_ref, bf16[512,768]{1,0:T(8,128)(2,1)S(1)} %bitcast.19, ...), custom_call_target="tpu_custom_call" | custom-call | flops 4899999744 | bytes 14000000 | tf_op jit(solution)/shard_map/pallas_call | solution.py:70
  132.6 0.0 copy-start.1
  132.6 0.0 reduce-scatter.2.cloned.1.call-update
  132.7 25.2 %all_to_all.15 = bf16[32,16,768]{2,1,0:T(8,128)(2,1)S(1)} all-to-all(bf16[32,16,768]{2,1,0:T(8,128)(2,1)S(1)} %bitcast.21), channel_id=1, replica_groups=mesh['y'=8,'x'=4,'z'=8,'k'=2] {'y','x'}, dimensions={0} | all-to-all | bytes 1572864 | tf_op jit(solution)/shard_map/all_to_all | solution.py:118
  157.9 0.1 convert_reduce_fusion
  158.0 0.1 reshape.38
  158.1 0.1 copy.12
  158.2 0.1 reshape.39
  158.3 15.8 %all_to_all.16 = f32[8,16,96]{2,1,0:T(8,128)S(1)} all-to-all(f32[8,16,96]{2,1,0:T(8,128)S(1)} %reshape.39), channel_id=1, replica_groups=mesh['y'=8,'x'=4,'z'=8,'k'=2] {'z'}, dimensions={0} | all-to-all | bytes 98304 | tf_op jit(solution)/shard_map/all_to_all | solution.py:121
  174.1 0.7 broadcast_in_dim.43
  174.8 6.0 %all-to-all-start.2 = ((bf16[32,16,96]{2,1,0:T(8,128)(2,1)}), bf16[32,16,96]{2,1,0:T(8,128)(2,1)S(1)}, u32[]{:S(2)}, u32[]{:S(2)}) async-start(bf16[32,16,96]{2,1,0:T(8,128)(2,1)} %broadcast_in_dim.43), calls=%async_computation.3 | async-start | bytes 262144 | tf_op jit(solution)/shard_map/all_to_all | solution.py:123
  180.8 0.0 copy-done.1
  180.8 0.4 copy.13
  181.2 9.2 %all-to-all-done.2 = bf16[32,16,96]{2,1,0:T(8,128)(2,1)S(1)} async-done(((bf16[32,16,96]{2,1,0:T(8,128)(2,1)}), bf16[32,16,96]{2,1,0:T(8,128)(2,1)S(1)}, u32[]{:S(2)}, u32[]{:S(2)}) %all-to-all-start.2) | async-done | bytes 98336 | tf_op jit(solution)/shard_map/all_to_all | solution.py:123
  190.3 0.4 reshape.40
  190.7 0.3 bitcast_add_fusion
  191.0 0.9 copy.14
  192.0 0.0 reduce-scatter.2.cloned.1.call-done
  192.0 0.9 convert_negate_fusion
  192.9 0.7 fusion
  (3 shorter events, 0.0 us)
Async XLA Ops:
  7.2 115.0 %all-gather.6.cloned.1.call-start = ((), (), s32[]{:S(2)}) async-start(), calls=%async_computation.5 | async-start | bytes 4866048 | tf_op jit(solution)/shard_map/all_gather | solution.py:108
  9.9 13.6 %collective-permute-start = (bf16[96,768]{1,0:T(8,128)(2,1)S(1)}, bf16[96,768]{1,0:T(8,128)(2,1)S(1)}, u32[]{:S(2)}, u32[]{:S(2)}) collective-permute-start(bf16[96,768]{1,0:T(8,128)(2,1)S(1)} %bitcast.25), channel_id=1, source_target_pairs={{0,0},{1,1},{2,64},{3,65},{4,128},{5,129},{6,192},{7,193},{8,256},... | collective-permute-start | bytes 442376 | tf_op jit(solution)/shard_map/ppermute | solution.py:107
  23.5 0.7 copy-start.2
  24.2 167.8 %reduce-scatter.2.cloned.1.call-start = ((), (), s32[]{:S(2)}) async-start(), calls=%async_computation.4 | async-start | bytes 1327104 | tf_op jit(solution)/shard_map/reduce_scatter | solution.py:114
  24.2 68.2 %collective-permute-start.1 = (bf16[768,1536]{1,0:T(8,128)(2,1)}, bf16[768,1536]{1,0:T(8,128)(2,1)}, u32[]{:S(2)}, u32[]{:S(2)}) collective-permute-start(bf16[768,1536]{1,0:T(8,128)(2,1)} %own_ref.1), channel_id=1, source_target_pairs={{0,1},{1,0},{2,3},{3,2},{4,5},{5,4},{6,7},{7,6},{8,9},{9,8},{10,11... | collective-permute-start | bytes 7077896 | tf_op jit(solution)/shard_map/ppermute | solution.py:99
  122.1 1.7 copy-start
  132.6 48.1 %copy-start.1 = (f32[3,512,32]{1,2,0:T(8,128)S(1)}, f32[3,512,32]{1,2,0:T(8,128)}, u32[]{:S(2)}) copy-start(f32[3,512,32]{1,2,0:T(8,128)} %param.7) | copy-start | bytes 589828
  174.8 15.6 %all-to-all-start.2 = ((bf16[32,16,96]{2,1,0:T(8,128)(2,1)}), bf16[32,16,96]{2,1,0:T(8,128)(2,1)S(1)}, u32[]{:S(2)}, u32[]{:S(2)}) async-start(bf16[32,16,96]{2,1,0:T(8,128)(2,1)} %broadcast_in_dim.43), calls=%async_computation.3 | async-start | bytes 262144 | tf_op jit(solution)/shard_map/all_to_all | solution.py:123
Sparse Core Ops, SparseCore 0:
  24.3 97.7 all-gather.5
  132.8 40.4 reduce-scatter.1

commit v2 on v1

v2 whole, which is shorter than its diff:
```python
import jax
import jax.numpy as jnp
from jax import lax
from jax.experimental import pallas as pl
from jax.experimental.pallas import tpu as pltpu
from jax.sharding import Mesh, PartitionSpec as P

AXES = ("y", "x", "z", "k")
ROW, COL = ("y", "x"), ("z", "k")
NY, NX, NZ, NK = 8, 4, 8, 2
SUPERS = 3
W = 512
WL = 32
SL = SUPERS * WL
ROWS = 768
SLOTS = 3
TB = 256
NT_DIMS = (((1,), (1,)), ((), ()))


def linear(y, x, z, k):
    return ((y * NX + x) * NZ + z) * NK + k


def permutation(f):
    pairs = []
    for y in range(NY):
        for x in range(NX):
            for z in range(NZ):
                for k in range(NK):
                    pairs.append((linear(y, x, z, k), linear(*f(y, x, z, k))))
    return pairs


def to_plane(y, x, z, k):
    return (-z - y) % NY, x, y, k


def to_sibling(y, x, z, k):
    return y, x, z, 1 - k


def product_kernel(where, gathered, own, sib, m0, m1, m2, part_ref, diag_ref, g_v, r_v, m_v, acc, g_sem, r_sem, m_sem):
    core, plane = where[0], where[1]
    g_copies, r_copies = [], []
    for s in range(4):
        x = 2 * (core ^ (s // 2)) + s % 2
        block = (own, sib)[s // 2].at[:, pl.ds(s % 2 * ROWS, ROWS)]
        g_copies.append(pltpu.make_async_copy(gathered.at[:, x], g_v.at[s], g_sem.at[s]))
        r_copies.append(pltpu.make_async_copy(block, r_v.at[s], r_sem.at[s]))
        g_copies[s].start()
        r_copies[s].start()
    m_copies = [pltpu.make_async_copy(m, m_v.at[j], m_sem.at[j]) for j, m in enumerate((m0, m1, m2))]
    for copy in m_copies:
        copy.start()
    for s in range(4):
        g_copies[s].wait()
        r_copies[s].wait()
        product = lax.dot_general(g_v[s].reshape(NY * SL, ROWS), r_v[s], NT_DIMS, preferred_element_type=jnp.float32)
        if s == 0:
            acc[...] = product
        elif s < 3:
            acc[...] += product
        else:
            total = (acc[...] + product).astype(jnp.bfloat16).reshape(NY, SL, ROWS)
            for y in range(NY):
                part_ref[lax.rem(2 * NY - y - plane, NZ)] = total[y]
    for j in range(SUPERS):
        m_copies[j].wait()
        mine = part_ref[:, j * WL:(j + 1) * WL, :].reshape(NZ * WL, ROWS)
        diag = lax.dot_general(m_v[j].reshape(W, ROWS), mine, NT_DIMS, preferred_element_type=jnp.float32)
        diag_ref[:, j * NZ * WL:(j + 1) * NZ * WL] = diag.astype(jnp.bfloat16)


def products(where, *arrays):
    return pl.pallas_call(
        product_kernel,
        in_specs=[pl.BlockSpec(memory_space=pltpu.SMEM)] + [pl.BlockSpec(memory_space=pl.ANY)] * 6,
        out_specs=[pl.BlockSpec(memory_space=pltpu.VMEM)] * 2,
        scratch_shapes=[
            pltpu.VMEM((4, NY, SL, ROWS), jnp.bfloat16),
            pltpu.VMEM((4, ROWS, ROWS), jnp.bfloat16),
            pltpu.VMEM((SUPERS, NZ * NK, WL, ROWS), jnp.bfloat16),
            pltpu.VMEM((NY * SL, ROWS), jnp.float32),
            pltpu.SemaphoreType.DMA((4,)),
            pltpu.SemaphoreType.DMA((4,)),
            pltpu.SemaphoreType.DMA((SUPERS,)),
        ],
        out_shape=[
            jax.ShapeDtypeStruct((NZ, SL, ROWS), jnp.bfloat16),
            jax.ShapeDtypeStruct((W, SUPERS * NZ * WL), jnp.bfloat16),
        ],
        compiler_params=pltpu.CompilerParams(vmem_limit_bytes=56 * 1024 * 1024),
        cost_estimate=pl.CostEstimate(flops=4_800_000_000, bytes_accessed=14_000_000, transcendentals=0),
    )(where, *arrays)


def on_device(resident, factor, diag_inverse, anc_tiles, slot_tile):
    y, x, z, k = (lax.axis_index(a) for a in AXES)

    turned = factor.transpose(0, 2, 1)
    arrived = lax.ppermute(turned.reshape(SL, ROWS), AXES, permutation(to_plane))
    sib = lax.ppermute(resident, AXES, permutation(to_sibling))

    def mask_of(block):
        slots = lax.dynamic_slice(slot_tile, (block * SLOTS,), (SLOTS,))
        listed = jnp.any(anc_tiles[:, None, :] == slots[None, :, None], axis=2)
        return jnp.repeat(listed, TB, axis=1)[:, None, :]

    mask = mask_of(y * NX + x)
    masked = jnp.where(mask, turned, jnp.bfloat16(0))
    rows = [lax.all_gather(masked[j], COL, axis=0, tiled=False) for j in range(SUPERS)]

    moved = jnp.where(mask_of(z * NX + x), arrived.reshape(SUPERS, WL, ROWS), jnp.bfloat16(0)).reshape(SL, ROWS)
    near = lax.all_gather(moved, "x", axis=0, tiled=False)
    gathered = lax.all_gather(near, "y", axis=0, tiled=False)

    part, diag = products(jnp.stack([k, z]).astype(jnp.int32), gathered, resident, sib, *rows)

    summed = lax.psum_scatter(part.reshape(NZ * SL, ROWS), "z", scatter_dimension=0, tiled=True)
    summed = summed.reshape(SUPERS, WL, ROWS).astype(jnp.float32)
    new_cols = jnp.where(mask, -summed, 0.0).astype(jnp.bfloat16).transpose(0, 2, 1)

    spread = lax.all_to_all(diag.reshape(NY * NX, W // (NY * NX), SUPERS * NZ * WL), ROW, 0, 0, tiled=True)
    slab = jnp.sum(spread.astype(jnp.float32), axis=0).reshape(W // (NY * NX), SUPERS, NZ, WL)
    slab = slab.transpose(2, 0, 1, 3).reshape(NZ, W // (NY * NX), SL)
    slab = jnp.sum(lax.all_to_all(slab, "z", 0, 0, tiled=True), axis=0).astype(jnp.bfloat16)
    copies = jnp.broadcast_to(slab[None], (NY * NX,) + slab.shape)
    total = lax.all_to_all(copies, ROW, 0, 0, tiled=True)
    total = total.reshape(W, SUPERS, WL).transpose(1, 0, 2).astype(jnp.float32)
    return new_cols, diag_inverse + total


def solution(mesh):
    fine = Mesh(mesh.devices.reshape(NY, NX, NZ, NK), AXES)
    return jax.shard_map(
        on_device,
        mesh=fine,
        in_specs=(P(ROW, COL), P(None, ROW, COL), P(None, None, COL), P(), P()),
        out_specs=(P(None, ROW, COL), P(None, None, COL)),
        check_vma=False,
    )
```

time: 201 us -> 187 us (0.930)
  waiting for transfers between devices: 48.3 us -> 20 us
  blocking collectives: 106 us -> 117 us
  starting transfers between devices: 12.2 us -> 15.2 us
    all_gather x1, waiting for transfers between devices: 29.7 us -> 0.01 us  [on_device(): gathered = lax.all_gather(near, 'y', axis=0, tiled=False)]
    all_gather x3 -> x4, blocking collectives: 65.3 us -> 75 us  [the longest x3 61 us: on_device(): lax.all_gather(masked[j], COL, axis=0, tiled=False)]
    all_to_all x1, blocking collectives: 25.2 us -> 28.9 us  [on_device(): lax.all_to_all(diag.reshape(NY * NX, W // (NY * NX), SUPERS * NZ * WL), R...]
    ppermute x2, starting transfers between devices: 6.09 us -> 9 us  [the longest x1 7.07 us: on_device(): lax.ppermute(turned.reshape(SL, ROWS), AXES, permutation(to_plane))]
    all_to_all x1, blocking collectives: 15.8 us -> 13 us  [on_device(): lax.all_to_all(slab, 'z', 0, 0, tiled=True)]
  transfers between devices with their start and end apart: 5 -> 5, of which waited for: 3 -> 2; matrix products, arithmetic and copies ran while one was open for 2% -> 3% of each run, Pallas kernels for 0% -> 0%
where the time goes in v2:
time: 187 us; the launch traced here: 186 us
  blocking collectives  117 us (63%)
  waiting for transfers between devices  20 us (11%)
  starting transfers between devices  15.2 us (8%)
  between operations  14.2 us (8%)
  Pallas kernels  10.6 us (6%)
  local copies, waits for them, and re-layouts  5.08 us (3%)
  other arithmetic  4.53 us (2%)
    all_gather x3, blocking collectives, on_device(): lax.all_gather(masked[j], COL, axis=0, tiled=False)  61 us
    all_to_all x1, blocking collectives, on_device(): lax.all_to_all(diag.reshape(NY * NX, W // (NY * NX), SUPERS * NZ * WL), R...  28.9 us
    all_gather x1, blocking collectives, on_device(): near = lax.all_gather(moved, 'x', axis=0, tiled=False)  14 us
    all_to_all x1, blocking collectives, on_device(): lax.all_to_all(slab, 'z', 0, 0, tiled=True)  13 us
    ppermute x1, waiting for transfers between devices, on_device(): lax.ppermute(turned.reshape(SL, ROWS), AXES, permutation(to_plane))  10.8 us
    pallas_call x1, Pallas kernels, products(): pl.pallas_call(product_kernel, in_specs=[pl.BlockSpec(memory_space=pltpu....  10.6 us
    all_to_all x1, waiting for transfers between devices, on_device(): total = lax.all_to_all(copies, ROW, 0, 0, tiled=True)  9.15 us
    ppermute x1, starting transfers between devices, on_device(): lax.ppermute(turned.reshape(SL, ROWS), AXES, permutation(to_plane))  7.07 us
  transfers between devices with their start and end apart: 5, of which 2 were waited for; matrix products, arithmetic and copies ran while one was open for 3% of the time, Pallas kernels for 0%

profile of v2, /device:TPU:8, one launch (start us, length us, event | category | flops | bytes accessed | tf_op | source)
XLA Modules:
  0.0 186.5 jit_solution(2700797898253519796)
XLA Ops:
  7.2 0.0 all-gather.4.cloned.1.call-start
  7.2 7.1 %collective-permute-start = (bf16[96,768]{1,0:T(8,128)(2,1)}, bf16[96,768]{1,0:T(8,128)(2,1)S(1)}, u32[]{:S(2)}, u32[]{:S(2)}) collective-permute-start(bf16[96,768]{1,0:T(8,128)(2,1)} %bitcast.29), channel_id=1, source_target_pairs={{0,0},{1,1},{2,448},{3,449},{4,384},{5,385},{6,320},{7,321},{8,256... | collective-permute-start | bytes 442376 | tf_op jit(solution)/shard_map/ppermute | solution.py:102
  14.3 0.8 fusion.2
  15.1 0.9 compare_reduce_fusion.1
  16.0 0.1 broadcast_bitcast_fusion
  16.1 10.8 %collective-permute-done = bf16[96,768]{1,0:T(8,128)(2,1)S(1)} collective-permute-done((bf16[96,768]{1,0:T(8,128)(2,1)}, bf16[96,768]{1,0:T(8,128)(2,1)S(1)}, u32[]{:S(2)}, u32[]{:S(2)}) %collective-permute-start) | collective-permute-done | bytes 147488 | tf_op jit(solution)/shard_map/ppermute | solution.py:102
  26.9 14.0 %all-gather = bf16[384,768]{1,0:T(8,128)(2,1)} all-gather(bf16[96,768]{1,0:T(8,128)(2,1)S(1)} %bitcast_select_fusion), channel_id=2, replica_groups=mesh['y'=8,'x'=4,'z'=8,'k'=2] {'x'}, dimensions={0}, use_global_device_ids=true | all-gather | bytes 737280 | tf_op jit(solution)/shard_map/all_gather | solution.py:115
  40.9 0.0 all-gather.4.cloned.1.call-update
  41.0 0.0 reduce-scatter.2.cloned.1.call-start
  41.0 1.9 %collective-permute-start.1 = (bf16[768,1536]{1,0:T(8,128)(2,1)}, bf16[768,1536]{1,0:T(8,128)(2,1)S(1)}, u32[]{:S(2)}, u32[]{:S(2)}) collective-permute-start(bf16[768,1536]{1,0:T(8,128)(2,1)} %own.1), channel_id=1, source_target_pairs={{0,1},{1,0},{2,3},{3,2},{4,5},{5,4},{6,7},{7,6},{8,9},{9,8},{10,11... | collective-permute-start | bytes 7077896 | tf_op jit(solution)/shard_map/ppermute | solution.py:103
  42.9 0.6 pad_add_fusion.where
  43.6 0.9 bitcast_select_fusion.1
  44.5 23.7 %all_gather.21.m0 = bf16[16,32,768]{2,1,0:T(8,128)(2,1)} all-gather(bf16[1,32,768]{2,1,0:T(8,128)(2,1)S(1)} %get-tuple-element.18), channel_id=1, replica_groups=mesh['y'=8,'x'=4,'z'=8,'k'=2] {'z','k'}, dimensions={0}, use_global_device_ids=true | all-gather | bytes 835584 | tf_op jit(solution)/shard_map/all_gather | solution.py:112
  68.2 18.0 %all_gather.22.m1 = bf16[16,32,768]{2,1,0:T(8,128)(2,1)} all-gather(bf16[1,32,768]{2,1,0:T(8,128)(2,1)S(1)} %get-tuple-element.17), channel_id=1, replica_groups=mesh['y'=8,'x'=4,'z'=8,'k'=2] {'z','k'}, dimensions={0}, use_global_device_ids=true | all-gather | bytes 835584 | tf_op jit(solution)/shard_map/all_gather | solution.py:112
  86.2 19.3 %all_gather.23.m2 = bf16[16,32,768]{2,1,0:T(8,128)(2,1)} all-gather(bf16[1,32,768]{2,1,0:T(8,128)(2,1)S(1)} %get-tuple-element.16), channel_id=1, replica_groups=mesh['y'=8,'x'=4,'z'=8,'k'=2] {'z','k'}, dimensions={0}, use_global_device_ids=true | all-gather | bytes 835584 | tf_op jit(solution)/shard_map/all_gather | solution.py:112
  105.6 0.0 collective-permute-done.1.sib
  105.6 0.0 copy-start.1
  105.6 0.0 all-gather.4.cloned.1.call-done
  105.6 1.4 copy-done.1
  107.0 10.6 %shard_map.68 = (bf16[8,96,768]{2,1,0:T(8,128)(2,1)}, bf16[512,768]{1,0:T(8,128)(2,1)}) custom-call(s32[2]{0:T(128)} %pad_add_fusion.where, bf16[8,4,96,768]{3,2,1,0:T(8,128)(2,1)} %bitcast.33, bf16[768,1536]{1,0:T(8,128)(2,1)} %own.1, bf16[768,1536]{1,0:T(8,128)(2,1)} %copy-done.1, bf16[16,32,768]{2,1,0:T(8,128)(2,1)} %all_gather.21.m0, ...), custom_call_target="tpu_custom_call" | custom-call | flops 4800000000 | bytes 14000000 | tf_op jit(solution)/shard_map/pallas_call | solution.py:76
  117.6 0.0 copy-start
  117.6 0.0 reduce-scatter.2.cloned.1.call-update
  117.6 28.9 %all_to_all.15 = bf16[32,16,768]{2,1,0:T(8,128)(2,1)S(1)} all-to-all(bf16[32,16,768]{2,1,0:T(8,128)(2,1)} %bitcast.26), channel_id=1, replica_groups=mesh['y'=8,'x'=4,'z'=8,'k'=2] {'y','x'}, dimensions={0} | all-to-all | bytes 1572864 | tf_op jit(solution)/shard_map/all_to_all | solution.py:124
  146.5 0.1 convert_reduce_fusion
  146.6 0.1 reshape.43
  146.7 0.1 copy.15
  146.8 0.1 reshape.44
  146.9 13.0 %all_to_all.16 = f32[8,16,96]{2,1,0:T(8,128)S(1)} all-to-all(f32[8,16,96]{2,1,0:T(8,128)S(1)} %reshape.44), channel_id=1, replica_groups=mesh['y'=8,'x'=4,'z'=8,'k'=2] {'z'}, dimensions={0} | all-to-all | bytes 98304 | tf_op jit(solution)/shard_map/all_to_all | solution.py:127
  160.0 0.7 broadcast_in_dim.62
  160.6 6.2 %all-to-all-start.2 = ((bf16[32,16,96]{2,1,0:T(8,128)(2,1)}), bf16[32,16,96]{2,1,0:T(8,128)(2,1)S(1)}, u32[]{:S(2)}, u32[]{:S(2)}) async-start(bf16[32,16,96]{2,1,0:T(8,128)(2,1)} %broadcast_in_dim.62), calls=%async_computation.3 | async-start | bytes 262144 | tf_op jit(solution)/shard_map/all_to_all | solution.py:129
  166.8 0.0 copy-done
  166.8 0.4 copy.16
  167.2 9.2 %all-to-all-done.2 = bf16[32,16,96]{2,1,0:T(8,128)(2,1)S(1)} async-done(((bf16[32,16,96]{2,1,0:T(8,128)(2,1)}), bf16[32,16,96]{2,1,0:T(8,128)(2,1)S(1)}, u32[]{:S(2)}, u32[]{:S(2)}) %all-to-all-start.2) | async-done | bytes 98336 | tf_op jit(solution)/shard_map/all_to_all | solution.py:129
  176.4 0.4 reshape.45
  176.8 0.3 bitcast_add_fusion
  177.1 0.9 copy.17
  178.0 0.0 reduce-scatter.2.cloned.1.call-done
  178.0 0.9 convert_negate_fusion
  179.0 0.7 fusion
  (5 shorter events, 0.1 us)
Async XLA Ops:
  7.2 98.4 %all-gather.4.cloned.1.call-start = ((), (), s32[]{:S(2)}) async-start(), calls=%async_computation.5 | async-start | bytes 5308416 | tf_op jit(solution)/shard_map/all_gather | solution.py:116
  7.2 19.7 %collective-permute-start = (bf16[96,768]{1,0:T(8,128)(2,1)}, bf16[96,768]{1,0:T(8,128)(2,1)S(1)}, u32[]{:S(2)}, u32[]{:S(2)}) collective-permute-start(bf16[96,768]{1,0:T(8,128)(2,1)} %bitcast.29), channel_id=1, source_target_pairs={{0,0},{1,1},{2,448},{3,449},{4,384},{5,385},{6,320},{7,321},{8,256... | collective-permute-start | bytes 442376 | tf_op jit(solution)/shard_map/ppermute | solution.py:102
  41.0 137.1 %reduce-scatter.2.cloned.1.call-start = ((), (), s32[]{:S(2)}) async-start(), calls=%async_computation.4 | async-start | bytes 1327104 | tf_op jit(solution)/shard_map/reduce_scatter | solution.py:120
  41.0 64.6 %collective-permute-start.1 = (bf16[768,1536]{1,0:T(8,128)(2,1)}, bf16[768,1536]{1,0:T(8,128)(2,1)S(1)}, u32[]{:S(2)}, u32[]{:S(2)}) collective-permute-start(bf16[768,1536]{1,0:T(8,128)(2,1)} %own.1), channel_id=1, source_target_pairs={{0,1},{1,0},{2,3},{3,2},{4,5},{5,4},{6,7},{7,6},{8,9},{9,8},{10,11... | collective-permute-start | bytes 7077896 | tf_op jit(solution)/shard_map/ppermute | solution.py:103
  105.6 1.4 copy-start.1
  117.6 49.2 %copy-start = (f32[3,512,32]{1,2,0:T(8,128)S(1)}, f32[3,512,32]{1,2,0:T(8,128)}, u32[]{:S(2)}) copy-start(f32[3,512,32]{1,2,0:T(8,128)} %param.7) | copy-start | bytes 589828
  160.6 15.7 %all-to-all-start.2 = ((bf16[32,16,96]{2,1,0:T(8,128)(2,1)}), bf16[32,16,96]{2,1,0:T(8,128)(2,1)S(1)}, u32[]{:S(2)}, u32[]{:S(2)}) async-start(bf16[32,16,96]{2,1,0:T(8,128)(2,1)} %broadcast_in_dim.62), calls=%async_computation.3 | async-start | bytes 262144 | tf_op jit(solution)/shard_map/all_to_all | solution.py:129
Sparse Core Ops, SparseCore 0:
  41.1 60.3 all-gather.3
  117.7 37.7 reduce-scatter.1

commit v3 on v2

--- a/solution.py
+++ b/solution.py
@@ -14,6 +14,8 @@
 SL = SUPERS * WL
 ROWS = 768
 SLOTS = 3
+CUT = 80
+PIECES = ((0, 0, 32, 0, 0), (0, 32, 32, 1, 0), (0, 64, 16, 2, 0), (1, 0, 16, 2, 16))
 TB = 256
 NT_DIMS = (((1,), (1,)), ((), ()))
 
@@ -40,9 +42,10 @@
     return y, x, z, 1 - k
 
 
-def product_kernel(where, gathered, own, sib, m0, m1, m2, part_ref, diag_ref, g_v, r_v, m_v, acc, g_sem, r_sem, m_sem):
+def product_kernel(where, gathered, own, sib, m_most, m_few, s_most, s_few, part_ref, diag_ref,
+                   g_v, r_v, m_v, acc, g_sem, r_sem, m_sem):
     core, plane = where[0], where[1]
-    g_copies, r_copies = [], []
+    g_copies, r_copies, m_copies = [], [], []
     for s in range(4):
         x = 2 * (core ^ (s // 2)) + s % 2
         block = (own, sib)[s // 2].at[:, pl.ds(s % 2 * ROWS, ROWS)]
@@ -50,9 +53,14 @@
         r_copies.append(pltpu.make_async_copy(block, r_v.at[s], r_sem.at[s]))
         g_copies[s].start()
         r_copies[s].start()
-    m_copies = [pltpu.make_async_copy(m, m_v.at[j], m_sem.at[j]) for j, m in enumerate((m0, m1, m2))]
-    for copy in m_copies:
-        copy.start()
+    for side, (many, rest) in enumerate(((m_most, m_few), (s_most, s_few))):
+        for i, (src, first, rows, j, at) in enumerate(PIECES):
+            m_copies.append(pltpu.make_async_copy(
+                (many, rest)[src].at[:, pl.ds(first, rows), :],
+                m_v.at[j, :, core ^ side, pl.ds(at, rows), :],
+                m_sem.at[len(PIECES) * side + i],
+            ))
+            m_copies[-1].start()
     for s in range(4):
         g_copies[s].wait()
         r_copies[s].wait()
@@ -65,8 +73,9 @@
             total = (acc[...] + product).astype(jnp.bfloat16).reshape(NY, SL, ROWS)
             for y in range(NY):
                 part_ref[lax.rem(2 * NY - y - plane, NZ)] = total[y]
+    for copy in m_copies:
+        copy.wait()
     for j in range(SUPERS):
-        m_copies[j].wait()
         mine = part_ref[:, j * WL:(j + 1) * WL, :].reshape(NZ * WL, ROWS)
         diag = lax.dot_general(m_v[j].reshape(W, ROWS), mine, NT_DIMS, preferred_element_type=jnp.float32)
         diag_ref[:, j * NZ * WL:(j + 1) * NZ * WL] = diag.astype(jnp.bfloat16)
@@ -75,16 +84,16 @@
 def products(where, *arrays):
     return pl.pallas_call(
         product_kernel,
-        in_specs=[pl.BlockSpec(memory_space=pltpu.SMEM)] + [pl.BlockSpec(memory_space=pl.ANY)] * 6,
+        in_specs=[pl.BlockSpec(memory_space=pltpu.SMEM)] + [pl.BlockSpec(memory_space=pl.ANY)] * 7,
         out_specs=[pl.BlockSpec(memory_space=pltpu.VMEM)] * 2,
         scratch_shapes=[
             pltpu.VMEM((4, NY, SL, ROWS), jnp.bfloat16),
             pltpu.VMEM((4, ROWS, ROWS), jnp.bfloat16),
-            pltpu.VMEM((SUPERS, NZ * NK, WL, ROWS), jnp.bfloat16),
+            pltpu.VMEM((SUPERS, NZ, NK, WL, ROWS), jnp.bfloat16),
             pltpu.VMEM((NY * SL, ROWS), jnp.float32),
             pltpu.SemaphoreType.DMA((4,)),
             pltpu.SemaphoreType.DMA((4,)),
-            pltpu.SemaphoreType.DMA((SUPERS,)),
+            pltpu.SemaphoreType.DMA((2 * len(PIECES),)),
         ],
         out_shape=[
             jax.ShapeDtypeStruct((NZ, SL, ROWS), jnp.bfloat16),
@@ -109,17 +118,24 @@
 
     mask = mask_of(y * NX + x)
     masked = jnp.where(mask, turned, jnp.bfloat16(0))
-    rows = [lax.all_gather(masked[j], COL, axis=0, tiled=False) for j in range(SUPERS)]
+    flat = masked.reshape(SL, ROWS)
+
+    def to_all(array, axis, size):
+        return lax.all_to_all(jnp.broadcast_to(array[None], (size,) + array.shape), axis, 0, 0, tiled=True)
+
+    m_few = to_all(flat[CUT:], "z", NZ)
+    m_most = lax.all_gather(flat[:CUT], "z", axis=0, tiled=False)
+    s_few = lax.ppermute(m_few, AXES, permutation(to_sibling))
+    s_most = lax.ppermute(m_most, AXES, permutation(to_sibling))
 
     moved = jnp.where(mask_of(z * NX + x), arrived.reshape(SUPERS, WL, ROWS), jnp.bfloat16(0)).reshape(SL, ROWS)
     near = lax.all_gather(moved, "x", axis=0, tiled=False)
     gathered = lax.all_gather(near, "y", axis=0, tiled=False)
 
-    part, diag = products(jnp.stack([k, z]).astype(jnp.int32), gathered, resident, sib, *rows)
+    part, diag = products(jnp.stack([k, z]).astype(jnp.int32), gathered, resident, sib, m_most, m_few, s_most, s_few)
 
     summed = lax.psum_scatter(part.reshape(NZ * SL, ROWS), "z", scatter_dimension=0, tiled=True)
-    summed = summed.reshape(SUPERS, WL, ROWS).astype(jnp.float32)
-    new_cols = jnp.where(mask, -summed, 0.0).astype(jnp.bfloat16).transpose(0, 2, 1)
+    new_cols = jnp.where(mask, -summed.reshape(SUPERS, WL, ROWS), jnp.bfloat16(0)).transpose(0, 2, 1)
 
     spread = lax.all_to_all(diag.reshape(NY * NX, W // (NY * NX), SUPERS * NZ * WL), ROW, 0, 0, tiled=True)
     slab = jnp.sum(spread.astype(jnp.float32), axis=0).reshape(W // (NY * NX), SUPERS, NZ, WL)
@@ -127,8 +143,8 @@
     slab = jnp.sum(lax.all_to_all(slab, "z", 0, 0, tiled=True), axis=0).astype(jnp.bfloat16)
     copies = jnp.broadcast_to(slab[None], (NY * NX,) + slab.shape)
     total = lax.all_to_all(copies, ROW, 0, 0, tiled=True)
-    total = total.reshape(W, SUPERS, WL).transpose(1, 0, 2).astype(jnp.float32)
-    return new_cols, diag_inverse + total
+    total = total.reshape(W, SL).T.reshape(SUPERS, WL, W).astype(jnp.float32)
+    return new_cols, (diag_inverse.transpose(0, 2, 1) + total).transpose(0, 2, 1)
 
 
 def solution(mesh):

time: 187 us -> 185 us (0.989)
  blocking collectives: 117 us -> 90 us
  waiting for transfers between devices: 20 us -> 41.3 us
  starting transfers between devices: 15.2 us -> 21.9 us
  local copies, waits for them, and re-layouts: 5.08 us -> 1.41 us
    all_gather x3 -> x1, blocking collectives: 61 us -> 29.6 us  [on_device(): m_most = lax.all_gather(flat[:CUT], 'z', axis=0, tiled=False)]
    all_to_all x1, waiting for transfers between devices: 9.15 us -> 21.4 us  [on_device(): lax.all_to_all(diag.reshape(NY * NX, W // (NY * NX), SUPERS * NZ * WL), R...]
    all_gather x1, waiting for transfers between devices: 0.01 us -> 7.46 us  [on_device(): gathered = lax.all_gather(near, 'y', axis=0, tiled=False)]
    ppermute x0 -> x2, starting transfers between devices: none -> 3.82 us  [the longest x1 1.91 us: on_device(): s_most = lax.ppermute(m_most, AXES, permutation(to_sibling))]
    all_to_all x1, blocking collectives: 13 us -> 15.9 us  [on_device(): lax.all_to_all(slab, 'z', 0, 0, tiled=True)]
    all_to_all x1, starting transfers between devices: 6.17 us -> 8.97 us  [on_device(): lax.all_to_all(diag.reshape(NY * NX, W // (NY * NX), SUPERS * NZ * WL), R...]
    unnamed x9 -> x11, local copies, waits for them, and re-layouts: 2.86 us -> 0.11 us
    all_to_all x1 -> x2, blocking collectives: 28.9 us -> 30.5 us  [the longest x1 15.3 us: on_device(): total = lax.all_to_all(copies, ROW, 0, 0, tiled=True)]
  transfers between devices with their start and end apart: 5 -> 7, of which waited for: 2 -> 4; matrix products, arithmetic and copies ran while one was open for 3% -> 3% of each run, Pallas kernels for 0% -> 0%
where the time goes in v3:
time: 185 us; the launch traced here: 184 us
  blocking collectives  90 us (49%)
  waiting for transfers between devices  41.3 us (22%)
  starting transfers between devices  21.9 us (12%)
  between operations  14.2 us (8%)
  Pallas kernels  10.6 us (6%)
  other arithmetic  4.95 us (3%)
    all_gather x1, blocking collectives, on_device(): m_most = lax.all_gather(flat[:CUT], 'z', axis=0, tiled=False)  29.6 us
    all_to_all x1, waiting for transfers between devices, on_device(): lax.all_to_all(diag.reshape(NY * NX, W // (NY * NX), SUPERS * NZ * WL), R...  21.4 us
    all_to_all x1, blocking collectives, on_device(): lax.all_to_all(slab, 'z', 0, 0, tiled=True)  15.9 us
    all_to_all x1, blocking collectives, on_device(): total = lax.all_to_all(copies, ROW, 0, 0, tiled=True)  15.3 us
    all_to_all x1, blocking collectives, to_all(): lax.all_to_all(jnp.broadcast_to(array[None], (size,) + array.shape), axis...  15.2 us
    all_gather x1, blocking collectives, on_device(): near = lax.all_gather(moved, 'x', axis=0, tiled=False)  14 us
    ppermute x1, waiting for transfers between devices, on_device(): lax.ppermute(turned.reshape(SL, ROWS), AXES, permutation(to_plane))  10.8 us
    pallas_call x1, Pallas kernels, products(): pl.pallas_call(product_kernel, in_specs=[pl.BlockSpec(memory_space=pltpu....  10.6 us
  transfers between devices with their start and end apart: 7, of which 4 were waited for; matrix products, arithmetic and copies ran while one was open for 3% of the time, Pallas kernels for 0%

profile of v3, /device:TPU:8, one launch (start us, length us, event | category | flops | bytes accessed | tf_op | source)
XLA Modules:
  0.0 184.4 jit_solution(5791143264678912576)
XLA Ops:
  7.2 0.0 all-gather.5.cloned.1.call-start
  7.2 7.1 %collective-permute-start = (bf16[96,768]{1,0:T(8,128)(2,1)}, bf16[96,768]{1,0:T(8,128)(2,1)S(1)}, u32[]{:S(2)}, u32[]{:S(2)}) collective-permute-start(bf16[96,768]{1,0:T(8,128)(2,1)} %bitcast.46), channel_id=1, source_target_pairs={{0,0},{1,1},{2,448},{3,449},{4,384},{5,385},{6,320},{7,321},{8,256... | collective-permute-start | bytes 442376 | tf_op jit(solution)/shard_map/ppermute | solution.py:111
  14.3 0.8 fusion.1
  15.1 0.9 compare_reduce_fusion.1
  16.0 0.1 broadcast_bitcast_fusion
  16.1 10.8 %collective-permute-done = bf16[96,768]{1,0:T(8,128)(2,1)S(1)} collective-permute-done((bf16[96,768]{1,0:T(8,128)(2,1)}, bf16[96,768]{1,0:T(8,128)(2,1)S(1)}, u32[]{:S(2)}, u32[]{:S(2)}) %collective-permute-start) | collective-permute-done | bytes 147488 | tf_op jit(solution)/shard_map/ppermute | solution.py:111
  26.9 14.0 %all-gather = bf16[384,768]{1,0:T(8,128)(2,1)} all-gather(bf16[96,768]{1,0:T(8,128)(2,1)S(1)} %bitcast_select_fusion), channel_id=2, replica_groups=mesh['y'=8,'x'=4,'z'=8,'k'=2] {'x'}, dimensions={0}, use_global_device_ids=true | all-gather | bytes 737280 | tf_op jit(solution)/shard_map/all_gather | solution.py:132
  40.9 0.0 all-gather.5.cloned.1.call-update
  41.0 1.9 %collective-permute-start.1 = (bf16[768,1536]{1,0:T(8,128)(2,1)}, bf16[768,1536]{1,0:T(8,128)(2,1)S(1)}, u32[]{:S(2)}, u32[]{:S(2)}) collective-permute-start(bf16[768,1536]{1,0:T(8,128)(2,1)} %own.1), channel_id=1, source_target_pairs={{0,1},{1,0},{2,3},{3,2},{4,5},{5,4},{6,7},{7,6},{8,9},{9,8},{10,11... | collective-permute-start | bytes 7077896 | tf_op jit(solution)/shard_map/ppermute | solution.py:112
  42.9 0.9 bitcast_select_fusion.1
  43.9 29.6 %all-gather.2 = bf16[640,768]{1,0:T(8,128)(2,1)S(1)} all-gather(bf16[80,768]{1,0:T(8,128)(2,1)S(1)} %slice.8), channel_id=4, replica_groups=mesh['y'=8,'x'=4,'z'=8,'k'=2] {'z'}, dimensions={0}, use_global_device_ids=true | all-gather | bytes 1105920 | tf_op jit(solution)/shard_map/all_gather | solution.py:127
  73.4 0.0 copy-start
  73.4 1.9 %collective-permute-start.2 = (bf16[8,80,768]{2,1,0:T(8,128)(2,1)S(1)}, bf16[8,80,768]{2,1,0:T(8,128)(2,1)}, u32[]{:S(2)}, u32[]{:S(2)}) collective-permute-start(bf16[8,80,768]{2,1,0:T(8,128)(2,1)S(1)} %bitcast.38), channel_id=1, source_target_pairs={{0,1},{1,0},{2,3},{3,2},{4,5},{5,4},{6,7},{7,6},{8,9},{9,8},{10,11... | collective-permute-start | bytes 2949128 | tf_op jit(solution)/shard_map/ppermute | solution.py:129
  75.4 15.2 %all_to_all.20.m_few = bf16[8,16,768]{2,1,0:T(8,128)(2,1)S(1)} all-to-all(bf16[8,16,768]{2,1,0:T(8,128)(2,1)S(1)} %broadcast_in_dim.61), channel_id=1, replica_groups=mesh['y'=8,'x'=4,'z'=8,'k'=2] {'z'}, dimensions={0} | all-to-all | bytes 393216 | tf_op jit(solution)/shard_map/all_to_all | solution.py:124
  90.6 0.0 copy-start.1
  90.6 1.9 %collective-permute-start.3 = (bf16[8,16,768]{2,1,0:T(8,128)(2,1)S(1)}, bf16[8,16,768]{2,1,0:T(8,128)(2,1)}, u32[]{:S(2)}, u32[]{:S(2)}) collective-permute-start(bf16[8,16,768]{2,1,0:T(8,128)(2,1)S(1)} %all_to_all.20.m_few), channel_id=1, source_target_pairs={{0,1},{1,0},{2,3},{3,2},{4,5},{5,4},{6,7},{7,6},{8,9},{9,8},{10,11... | collective-permute-start | bytes 589832 | tf_op jit(solution)/shard_map/ppermute | solution.py:128
  92.5 0.6 pad_add_fusion.where
  93.1 0.9 collective-permute-done.3.s_few
  94.1 0.0 collective-permute-done.2.s_most
  94.1 0.0 collective-permute-done.1.sib
  94.1 0.0 copy-start.3
  94.1 7.5 %all-gather.5.cloned.1.call-done = bf16[32,96,768]{2,1,0:T(8,128)(2,1)} async-done(((bf16[4,96,768]{2,1,0:T(8,128)(2,1)}), bf16[32,96,768]{2,1,0:T(8,128)(2,1)}) %all-gather.5.cloned.1.call-update) | async-done | bytes 4718608 | tf_op jit(solution)/shard_map/all_gather | solution.py:133
  101.5 0.0 copy-done
  101.5 0.0 copy-done.1
  101.5 0.0 copy-done.3
  101.5 10.6 %shard_map.68 = (bf16[8,96,768]{2,1,0:T(8,128)(2,1)}, bf16[512,768]{1,0:T(8,128)(2,1)}) custom-call(s32[2]{0:T(128)} %pad_add_fusion.where, bf16[8,4,96,768]{3,2,1,0:T(8,128)(2,1)} %bitcast.50, bf16[768,1536]{1,0:T(8,128)(2,1)} %own.1, bf16[768,1536]{1,0:T(8,128)(2,1)} %copy-done.3, bf16[8,80,768]{2,1,0:T(8,128)(2,1)} %bitcast.39, ...), custom_call_target="tpu_custom_call" | custom-call | flops 4800000000 | bytes 14000000 | tf_op jit(solution)/shard_map/pallas_call | solution.py:85
  112.2 9.0 %all-to-all-start.1 = ((bf16[32,16,768]{2,1,0:T(8,128)(2,1)}), bf16[32,16,768]{2,1,0:T(8,128)(2,1)S(1)}, u32[]{:S(2)}, u32[]{:S(2)}) async-start(bf16[32,16,768]{2,1,0:T(8,128)(2,1)} %bitcast.40), calls=%async_computation.2 | async-start | bytes 1572864 | tf_op jit(solution)/shard_map/all_to_all | solution.py:140
  121.2 0.0 copy-start.2
  121.2 0.0 reduce-scatter.2.cloned.1.call-start
  121.2 0.7 reduce-scatter.2.cloned.1.call-update
  121.9 21.4 %all-to-all-done.1 = bf16[32,16,768]{2,1,0:T(8,128)(2,1)S(1)} async-done(((bf16[32,16,768]{2,1,0:T(8,128)(2,1)}), bf16[32,16,768]{2,1,0:T(8,128)(2,1)S(1)}, u32[]{:S(2)}, u32[]{:S(2)}) %all-to-all-start.1) | async-done | bytes 786464 | tf_op jit(solution)/shard_map/all_to_all | solution.py:140
  143.3 0.1 convert_reduce_fusion
  143.4 0.1 reshape.50
  143.6 0.1 copy.12
  143.6 0.1 reshape.51
  143.8 15.9 %all_to_all.21 = f32[8,16,96]{2,1,0:T(8,128)S(1)} all-to-all(f32[8,16,96]{2,1,0:T(8,128)S(1)} %reshape.51), channel_id=1, replica_groups=mesh['y'=8,'x'=4,'z'=8,'k'=2] {'z'}, dimensions={0} | all-to-all | bytes 98304 | tf_op jit(solution)/shard_map/all_to_all | solution.py:143
  159.8 15.3 %all_to_all.22 = bf16[32,16,96]{2,1,0:T(8,128)(2,1)S(1)} all-to-all(bf16[32,16,96]{2,1,0:T(8,128)(2,1)S(1)} %broadcast_in_dim.62), channel_id=1, replica_groups=mesh['y'=8,'x'=4,'z'=8,'k'=2] {'y','x'}, dimensions={0} | all-to-all | bytes 196608 | tf_op jit(solution)/shard_map/all_to_all | solution.py:145
  175.1 0.1 copy.13
  175.2 0.0 copy-done.2
  175.2 0.7 fusion
  175.9 0.0 reduce-scatter.2.cloned.1.call-done
  175.9 0.9 neg.6
  176.9 0.7 select_bitcast_fusion
  (9 shorter events, 0.1 us)
Async XLA Ops:
  7.2 94.4 %all-gather.5.cloned.1.call-start = ((), (), s32[]{:S(2)}) async-start(), calls=%async_computation.6 | async-start | bytes 5308416 | tf_op jit(solution)/shard_map/all_gather | solution.py:133
  7.2 19.7 %collective-permute-start = (bf16[96,768]{1,0:T(8,128)(2,1)}, bf16[96,768]{1,0:T(8,128)(2,1)S(1)}, u32[]{:S(2)}, u32[]{:S(2)}) collective-permute-start(bf16[96,768]{1,0:T(8,128)(2,1)} %bitcast.46), channel_id=1, source_target_pairs={{0,0},{1,1},{2,448},{3,449},{4,384},{5,385},{6,320},{7,321},{8,256... | collective-permute-start | bytes 442376 | tf_op jit(solution)/shard_map/ppermute | solution.py:111
  41.0 53.1 %collective-permute-start.1 = (bf16[768,1536]{1,0:T(8,128)(2,1)}, bf16[768,1536]{1,0:T(8,128)(2,1)S(1)}, u32[]{:S(2)}, u32[]{:S(2)}) collective-permute-start(bf16[768,1536]{1,0:T(8,128)(2,1)} %own.1), channel_id=1, source_target_pairs={{0,1},{1,0},{2,3},{3,2},{4,5},{5,4},{6,7},{7,6},{8,9},{9,8},{10,11... | collective-permute-start | bytes 7077896 | tf_op jit(solution)/shard_map/ppermute | solution.py:112
  73.4 28.1 %copy-start = (bf16[640,768]{1,0:T(8,128)(2,1)}, bf16[640,768]{1,0:T(8,128)(2,1)S(1)}, u32[]{:S(2)}) copy-start(bf16[640,768]{1,0:T(8,128)(2,1)S(1)} %all-gather.2) | copy-start | bytes 2949124
  73.4 20.6 %collective-permute-start.2 = (bf16[8,80,768]{2,1,0:T(8,128)(2,1)S(1)}, bf16[8,80,768]{2,1,0:T(8,128)(2,1)}, u32[]{:S(2)}, u32[]{:S(2)}) collective-permute-start(bf16[8,80,768]{2,1,0:T(8,128)(2,1)S(1)} %bitcast.38), channel_id=1, source_target_pairs={{0,1},{1,0},{2,3},{3,2},{4,5},{5,4},{6,7},{7,6},{8,9},{9,8},{10,11... | collective-permute-start | bytes 2949128 | tf_op jit(solution)/shard_map/ppermute | solution.py:129
  90.6 10.9 %copy-start.1 = (bf16[8,16,768]{2,1,0:T(8,128)(2,1)}, bf16[8,16,768]{2,1,0:T(8,128)(2,1)S(1)}, u32[]{:S(2)}) copy-start(bf16[8,16,768]{2,1,0:T(8,128)(2,1)S(1)} %all_to_all.20.m_few) | copy-start | bytes 589828
  90.6 3.5 %collective-permute-start.3 = (bf16[8,16,768]{2,1,0:T(8,128)(2,1)S(1)}, bf16[8,16,768]{2,1,0:T(8,128)(2,1)}, u32[]{:S(2)}, u32[]{:S(2)}) collective-permute-start(bf16[8,16,768]{2,1,0:T(8,128)(2,1)S(1)} %all_to_all.20.m_few), channel_id=1, source_target_pairs={{0,1},{1,0},{2,3},{3,2},{4,5},{5,4},{6,7},{7,6},{8,9},{9,8},{10,11... | collective-permute-start | bytes 589832 | tf_op jit(solution)/shard_map/ppermute | solution.py:128
  94.1 7.5 %copy-start.3 = (bf16[768,1536]{1,0:T(8,128)(2,1)}, bf16[768,1536]{1,0:T(8,128)(2,1)S(1)}, u32[]{:S(2)}) copy-start(bf16[768,1536]{1,0:T(8,128)(2,1)S(1)} %collective-permute-done.1.sib) | copy-start | bytes 7077892
  112.2 31.2 %all-to-all-start.1 = ((bf16[32,16,768]{2,1,0:T(8,128)(2,1)}), bf16[32,16,768]{2,1,0:T(8,128)(2,1)S(1)}, u32[]{:S(2)}, u32[]{:S(2)}) async-start(bf16[32,16,768]{2,1,0:T(8,128)(2,1)} %bitcast.40), calls=%async_computation.2 | async-start | bytes 1572864 | tf_op jit(solution)/shard_map/all_to_all | solution.py:140
  121.2 54.1 %copy-start.2 = (f32[3,512,32]{1,2,0:T(8,128)S(1)}, f32[3,512,32]{1,2,0:T(8,128)}, u32[]{:S(2)}) copy-start(f32[3,512,32]{1,2,0:T(8,128)} %param.7) | copy-start | bytes 589828
  121.2 54.8 %reduce-scatter.2.cloned.1.call-start = ((), (), s32[]{:S(2)}) async-start(), calls=%async_computation.5 | async-start | bytes 1327104 | tf_op jit(solution)/shard_map/reduce_scatter | solution.py:137
Sparse Core Ops, SparseCore 0:
  41.1 60.3 all-gather.4
  124.8 44.1 reduce-scatter.1

commit v4 on v3

--- a/solution.py
+++ b/solution.py
@@ -129,7 +129,7 @@
     s_most = lax.ppermute(m_most, AXES, permutation(to_sibling))
 
     moved = jnp.where(mask_of(z * NX + x), arrived.reshape(SUPERS, WL, ROWS), jnp.bfloat16(0)).reshape(SL, ROWS)
-    near = lax.all_gather(moved, "x", axis=0, tiled=False)
+    near = to_all(moved, "x", NX)
     gathered = lax.all_gather(near, "y", axis=0, tiled=False)
 
     part, diag = products(jnp.stack([k, z]).astype(jnp.int32), gathered, resident, sib, m_most, m_few, s_most, s_few)

time: 185 us -> 183 us (0.989)
    all_gather x1 -> x0, blocking collectives: 14 us -> none  [on_device(): near = lax.all_gather(moved, 'x', axis=0, tiled=False)]
    all_to_all x1 -> x2, blocking collectives: 15.2 us -> 27.8 us  [to_all(): lax.all_to_all(jnp.broadcast_to(array[None], (size,) + array.shape), axis...]
  transfers between devices with their start and end apart: 7 -> 7, of which waited for: 4 -> 4; matrix products, arithmetic and copies ran while one was open for 3% -> 2% of each run, Pallas kernels for 0% -> 0%
where the time goes in v4:
time: 183 us; the launch traced here: 182 us
  blocking collectives  88.8 us (49%)
  waiting for transfers between devices  40.8 us (22%)
  starting transfers between devices  22 us (12%)
  between operations  14.3 us (8%)
  Pallas kernels  10.6 us (6%)
  other arithmetic  4.02 us (2%)
    all_gather x1, blocking collectives, on_device(): m_most = lax.all_gather(flat[:CUT], 'z', axis=0, tiled=False)  29.7 us
    all_to_all x2, blocking collectives, to_all(): lax.all_to_all(jnp.broadcast_to(array[None], (size,) + array.shape), axis...  27.8 us
    all_to_all x1, waiting for transfers between devices, on_device(): lax.all_to_all(diag.reshape(NY * NX, W // (NY * NX), SUPERS * NZ * WL), R...  21.4 us
    all_to_all x1, blocking collectives, on_device(): lax.all_to_all(slab, 'z', 0, 0, tiled=True)  16 us
    all_to_all x1, blocking collectives, on_device(): total = lax.all_to_all(copies, ROW, 0, 0, tiled=True)  15.3 us
    ppermute x1, waiting for transfers between devices, on_device(): lax.ppermute(turned.reshape(SL, ROWS), AXES, permutation(to_plane))  10.8 us
    pallas_call x1, Pallas kernels, products(): pl.pallas_call(product_kernel, in_specs=[pl.BlockSpec(memory_space=pltpu....  10.6 us
    all_to_all x1, starting transfers between devices, on_device(): lax.all_to_all(diag.reshape(NY * NX, W // (NY * NX), SUPERS * NZ * WL), R...  8.97 us
  transfers between devices with their start and end apart: 7, of which 4 were waited for; matrix products, arithmetic and copies ran while one was open for 2% of the time, Pallas kernels for 0%

profile of v4, /device:TPU:8, one launch (start us, length us, event | category | flops | bytes accessed | tf_op | source)
XLA Modules:
  0.0 182.0 jit_solution(14457353794728400173)
XLA Ops:
  7.2 0.0 copy-start.3
  7.2 0.0 copy-start.4
  7.2 0.0 all-gather.4.cloned.1.call-start
  7.2 7.2 %collective-permute-start = (bf16[96,768]{1,0:T(8,128)(2,1)}, bf16[96,768]{1,0:T(8,128)(2,1)S(1)}, u32[]{:S(2)}, u32[]{:S(2)}) collective-permute-start(bf16[96,768]{1,0:T(8,128)(2,1)} %bitcast.44), channel_id=1, source_target_pairs={{0,0},{1,1},{2,448},{3,449},{4,384},{5,385},{6,320},{7,321},{8,256... | collective-permute-start | bytes 442376 | tf_op jit(solution)/shard_map/ppermute | solution.py:111
  14.5 0.8 fusion.1
  15.3 0.9 compare_reduce_fusion.1
  16.2 0.1 broadcast_bitcast_fusion
  16.3 10.8 %collective-permute-done = bf16[96,768]{1,0:T(8,128)(2,1)S(1)} collective-permute-done((bf16[96,768]{1,0:T(8,128)(2,1)}, bf16[96,768]{1,0:T(8,128)(2,1)S(1)}, u32[]{:S(2)}, u32[]{:S(2)}) %collective-permute-start) | collective-permute-done | bytes 147488 | tf_op jit(solution)/shard_map/ppermute | solution.py:111
  27.1 12.6 %all_to_all.25 = bf16[4,96,768]{2,1,0:T(8,128)(2,1)} all-to-all(bf16[4,96,768]{2,1,0:T(8,128)(2,1)S(1)} %broadcast_in_dim.65), channel_id=1, replica_groups=mesh['y'=8,'x'=4,'z'=8,'k'=2] {'x'}, dimensions={0} | all-to-all | bytes 1179648 | tf_op jit(solution)/shard_map/all_to_all | solution.py:124
  39.8 0.0 all-gather.4.cloned.1.call-update
  39.8 0.0 copy-done.4
  39.8 1.9 %collective-permute-start.1 = (bf16[768,1536]{1,0:T(8,128)(2,1)S(1)}, bf16[768,1536]{1,0:T(8,128)(2,1)}, u32[]{:S(2)}, u32[]{:S(2)}) collective-permute-start(bf16[768,1536]{1,0:T(8,128)(2,1)S(1)} %copy-done.4), channel_id=1, source_target_pairs={{0,1},{1,0},{2,3},{3,2},{4,5},{5,4},{6,7},{7,6},{8,9},{9,8},{10,11... | collective-permute-start | bytes 7077896 | tf_op jit(solution)/shard_map/ppermute | solution.py:112
  41.7 0.0 copy-done.3
  41.8 29.7 %all-gather.1 = bf16[640,768]{1,0:T(8,128)(2,1)S(1)} all-gather(bf16[80,768]{1,0:T(8,128)(2,1)S(1)} %slice.8), channel_id=3, replica_groups=mesh['y'=8,'x'=4,'z'=8,'k'=2] {'z'}, dimensions={0}, use_global_device_ids=true | all-gather | bytes 1105920 | tf_op jit(solution)/shard_map/all_gather | solution.py:127
  71.5 0.0 copy-start
  71.5 1.9 %collective-permute-start.2 = (bf16[8,80,768]{2,1,0:T(8,128)(2,1)S(1)}, bf16[8,80,768]{2,1,0:T(8,128)(2,1)}, u32[]{:S(2)}, u32[]{:S(2)}) collective-permute-start(bf16[8,80,768]{2,1,0:T(8,128)(2,1)S(1)} %bitcast.36), channel_id=1, source_target_pairs={{0,1},{1,0},{2,3},{3,2},{4,5},{5,4},{6,7},{7,6},{8,9},{9,8},{10,11... | collective-permute-start | bytes 2949128 | tf_op jit(solution)/shard_map/ppermute | solution.py:129
  73.4 15.2 %all_to_all.26.m_few = bf16[8,16,768]{2,1,0:T(8,128)(2,1)S(1)} all-to-all(bf16[8,16,768]{2,1,0:T(8,128)(2,1)S(1)} %broadcast_in_dim.67), channel_id=1, replica_groups=mesh['y'=8,'x'=4,'z'=8,'k'=2] {'z'}, dimensions={0} | all-to-all | bytes 393216 | tf_op jit(solution)/shard_map/all_to_all | solution.py:124
  88.7 0.0 copy-start.1
  88.7 1.9 %collective-permute-start.3 = (bf16[8,16,768]{2,1,0:T(8,128)(2,1)S(1)}, bf16[8,16,768]{2,1,0:T(8,128)(2,1)}, u32[]{:S(2)}, u32[]{:S(2)}) collective-permute-start(bf16[8,16,768]{2,1,0:T(8,128)(2,1)S(1)} %all_to_all.26.m_few), channel_id=1, source_target_pairs={{0,1},{1,0},{2,3},{3,2},{4,5},{5,4},{6,7},{7,6},{8,9},{9,8},{10,11... | collective-permute-start | bytes 589832 | tf_op jit(solution)/shard_map/ppermute | solution.py:128
  90.6 0.6 pad_add_fusion.where
  91.2 1.0 collective-permute-done.3.s_few
  92.1 0.0 collective-permute-done.2.s_most
  92.1 0.0 collective-permute-done.1.sib
  92.1 7.0 %all-gather.4.cloned.1.call-done = bf16[32,96,768]{2,1,0:T(8,128)(2,1)} async-done(((bf16[4,96,768]{2,1,0:T(8,128)(2,1)}), bf16[32,96,768]{2,1,0:T(8,128)(2,1)}) %all-gather.4.cloned.1.call-update) | async-done | bytes 4718608 | tf_op jit(solution)/shard_map/all_gather | solution.py:133
  99.1 0.0 copy-done
  99.1 0.0 copy-done.1
  99.1 10.6 %shard_map.68 = (bf16[8,96,768]{2,1,0:T(8,128)(2,1)}, bf16[512,768]{1,0:T(8,128)(2,1)}) custom-call(s32[2]{0:T(128)} %pad_add_fusion.where, bf16[8,4,96,768]{3,2,1,0:T(8,128)(2,1)} %bitcast.48, bf16[768,1536]{1,0:T(8,128)(2,1)} %own.1, bf16[768,1536]{1,0:T(8,128)(2,1)} %collective-permute-done.1.sib, bf16[8,80,768]{2,1,0:T(8,128)(2,1)} %bitcast.37, ...), custom_call_target="tpu_custom_call" | custom-call | flops 4800000000 | bytes 14000000 | tf_op jit(solution)/shard_map/pallas_call | solution.py:85
  109.8 9.0 %all-to-all-start.2 = ((bf16[32,16,768]{2,1,0:T(8,128)(2,1)}), bf16[32,16,768]{2,1,0:T(8,128)(2,1)S(1)}, u32[]{:S(2)}, u32[]{:S(2)}) async-start(bf16[32,16,768]{2,1,0:T(8,128)(2,1)} %bitcast.38), calls=%async_computation.3 | async-start | bytes 1572864 | tf_op jit(solution)/shard_map/all_to_all | solution.py:140
  118.7 0.0 copy-start.2
  118.8 0.0 reduce-scatter.2.cloned.1.call-start
  118.8 0.7 reduce-scatter.2.cloned.1.call-update
  119.5 21.4 %all-to-all-done.2 = bf16[32,16,768]{2,1,0:T(8,128)(2,1)S(1)} async-done(((bf16[32,16,768]{2,1,0:T(8,128)(2,1)}), bf16[32,16,768]{2,1,0:T(8,128)(2,1)S(1)}, u32[]{:S(2)}, u32[]{:S(2)}) %all-to-all-start.2) | async-done | bytes 786464 | tf_op jit(solution)/shard_map/all_to_all | solution.py:140
  140.9 0.1 convert_reduce_fusion
  141.0 0.1 reshape.51
  141.1 0.1 copy.12
  141.2 0.1 reshape.52
  141.4 16.0 %all_to_all.27 = f32[8,16,96]{2,1,0:T(8,128)S(1)} all-to-all(f32[8,16,96]{2,1,0:T(8,128)S(1)} %reshape.52), channel_id=1, replica_groups=mesh['y'=8,'x'=4,'z'=8,'k'=2] {'z'}, dimensions={0} | all-to-all | bytes 98304 | tf_op jit(solution)/shard_map/all_to_all | solution.py:143
  157.4 15.3 %all_to_all.28 = bf16[32,16,96]{2,1,0:T(8,128)(2,1)S(1)} all-to-all(bf16[32,16,96]{2,1,0:T(8,128)(2,1)S(1)} %broadcast_in_dim.68), channel_id=1, replica_groups=mesh['y'=8,'x'=4,'z'=8,'k'=2] {'y','x'}, dimensions={0} | all-to-all | bytes 196608 | tf_op jit(solution)/shard_map/all_to_all | solution.py:145
  172.7 0.1 copy.13
  172.8 0.0 copy-done.2
  172.8 0.7 fusion
  173.5 0.0 reduce-scatter.2.cloned.1.call-done
  173.5 0.9 neg.6
  174.5 0.7 select_bitcast_fusion
  (11 shorter events, 0.2 us)
Async XLA Ops:
  7.2 34.6 %copy-start.3 = (bf16[3,768,32]{1,2,0:T(8,128)(2,1)S(1)}, bf16[3,768,32]{1,2,0:T(8,128)(2,1)}, u32[]{:S(2)}) copy-start(bf16[3,768,32]{1,2,0:T(8,128)(2,1)} %param.6) | copy-start | bytes 442372
  7.2 32.6 %copy-start.4 = (bf16[768,1536]{1,0:T(8,128)(2,1)S(1)}, bf16[768,1536]{1,0:T(8,128)(2,1)}, u32[]{:S(2)}) copy-start(bf16[768,1536]{1,0:T(8,128)(2,1)} %own.1) | copy-start | bytes 7077892
  7.2 91.9 %all-gather.4.cloned.1.call-start = ((), (), s32[]{:S(2)}) async-start(), calls=%async_computation.7 | async-start | bytes 5308416 | tf_op jit(solution)/shard_map/all_gather | solution.py:133
  7.2 19.8 %collective-permute-start = (bf16[96,768]{1,0:T(8,128)(2,1)}, bf16[96,768]{1,0:T(8,128)(2,1)S(1)}, u32[]{:S(2)}, u32[]{:S(2)}) collective-permute-start(bf16[96,768]{1,0:T(8,128)(2,1)} %bitcast.44), channel_id=1, source_target_pairs={{0,0},{1,1},{2,448},{3,449},{4,384},{5,385},{6,320},{7,321},{8,256... | collective-permute-start | bytes 442376 | tf_op jit(solution)/shard_map/ppermute | solution.py:111
  39.8 52.3 %collective-permute-start.1 = (bf16[768,1536]{1,0:T(8,128)(2,1)S(1)}, bf16[768,1536]{1,0:T(8,128)(2,1)}, u32[]{:S(2)}, u32[]{:S(2)}) collective-permute-start(bf16[768,1536]{1,0:T(8,128)(2,1)S(1)} %copy-done.4), channel_id=1, source_target_pairs={{0,1},{1,0},{2,3},{3,2},{4,5},{5,4},{6,7},{7,6},{8,9},{9,8},{10,11... | collective-permute-start | bytes 7077896 | tf_op jit(solution)/shard_map/ppermute | solution.py:112
  71.5 27.6 %copy-start = (bf16[640,768]{1,0:T(8,128)(2,1)}, bf16[640,768]{1,0:T(8,128)(2,1)S(1)}, u32[]{:S(2)}) copy-start(bf16[640,768]{1,0:T(8,128)(2,1)S(1)} %all-gather.1) | copy-start | bytes 2949124
  71.5 20.6 %collective-permute-start.2 = (bf16[8,80,768]{2,1,0:T(8,128)(2,1)S(1)}, bf16[8,80,768]{2,1,0:T(8,128)(2,1)}, u32[]{:S(2)}, u32[]{:S(2)}) collective-permute-start(bf16[8,80,768]{2,1,0:T(8,128)(2,1)S(1)} %bitcast.36), channel_id=1, source_target_pairs={{0,1},{1,0},{2,3},{3,2},{4,5},{5,4},{6,7},{7,6},{8,9},{9,8},{10,11... | collective-permute-start | bytes 2949128 | tf_op jit(solution)/shard_map/ppermute | solution.py:129
  88.7 10.5 %copy-start.1 = (bf16[8,16,768]{2,1,0:T(8,128)(2,1)}, bf16[8,16,768]{2,1,0:T(8,128)(2,1)S(1)}, u32[]{:S(2)}) copy-start(bf16[8,16,768]{2,1,0:T(8,128)(2,1)S(1)} %all_to_all.26.m_few) | copy-start | bytes 589828
  88.7 3.5 %collective-permute-start.3 = (bf16[8,16,768]{2,1,0:T(8,128)(2,1)S(1)}, bf16[8,16,768]{2,1,0:T(8,128)(2,1)}, u32[]{:S(2)}, u32[]{:S(2)}) collective-permute-start(bf16[8,16,768]{2,1,0:T(8,128)(2,1)S(1)} %all_to_all.26.m_few), channel_id=1, source_target_pairs={{0,1},{1,0},{2,3},{3,2},{4,5},{5,4},{6,7},{7,6},{8,9},{9,8},{10,11... | collective-permute-start | bytes 589832 | tf_op jit(solution)/shard_map/ppermute | solution.py:128
  109.8 31.2 %all-to-all-start.2 = ((bf16[32,16,768]{2,1,0:T(8,128)(2,1)}), bf16[32,16,768]{2,1,0:T(8,128)(2,1)S(1)}, u32[]{:S(2)}, u32[]{:S(2)}) async-start(bf16[32,16,768]{2,1,0:T(8,128)(2,1)} %bitcast.38), calls=%async_computation.3 | async-start | bytes 1572864 | tf_op jit(solution)/shard_map/all_to_all | solution.py:140
  118.7 54.1 %copy-start.2 = (f32[3,512,32]{1,2,0:T(8,128)S(1)}, f32[3,512,32]{1,2,0:T(8,128)}, u32[]{:S(2)}) copy-start(f32[3,512,32]{1,2,0:T(8,128)} %param.7) | copy-start | bytes 589828
  118.8 54.8 %reduce-scatter.2.cloned.1.call-start = ((), (), s32[]{:S(2)}) async-start(), calls=%async_computation.6 | async-start | bytes 1327104 | tf_op jit(solution)/shard_map/reduce_scatter | solution.py:137
Sparse Core Ops, SparseCore 0:
  39.9 59.1 all-gather.3
  122.4 44.0 reduce-scatter.1
